TPU v7x, 32 devices: a whole 2x2x4 slice. The times are simulated.
32 devices in a mesh: dp: 8 (over z, y), expert: 4 (over x, core).
Axes of the slice: x: 2, y: 2, z: 4, core: 2. Of those that a mesh axis runs over, the one named last changes fastest.
Arguments:
- tokens: bfloat16 [4096, 2048], P(('dp', 'expert')), may hold values from -6 to 6
- choices: int32 [4096, 2], P(('dp', 'expert')), may hold values from 0 to 4, as said below
- gate_codes: int32 [4096, 2], P(('dp', 'expert')), may hold values from 16 to 255
- hot_list: int32 [8], P('dp'), may hold values from 0 to 3
- w_in: bfloat16 [4, 2048, 1024], P('expert'), may hold values from -0.125 to 0.125
- w_down: bfloat16 [4, 512, 2048], P('expert'), may hold values from -0.25 to 0.25
Outputs:
- mixed: bfloat16 [4096, 2048], P(('dp', 'expert'))
- expert_load: float32 [4], P('expert')
Inputs may be any that keep to these rules, and one draw needn't show every extreme that they name: `choices`: each row names two different values. The value 4 stands for the hot expert of the row's data group, whose own number never appears in that group's rows. The 128 rows of one device hold 4 exactly 16 times and any other value at most 80 times; on every device some value occurs exactly 80 times.
All inputs are finite; a program needn't handle non-finite values.
Results may differ from a plain program's by a relative error of at most 0.0057.
Values may be sent and summed in bfloat16 or wider, within the bound.
A program may use at most 64 MiB of HBM per device.

v0:
```python
import jax
import jax.numpy as jnp
from jax import lax
from jax.sharding import PartitionSpec as P


def expert_rows(row_block, weight_in, weight_down):
    projected = jnp.dot(row_block, weight_in, preferred_element_type=jnp.float32)
    hidden_width = weight_down.shape[0]
    hidden = (jax.nn.silu(projected[:, :hidden_width]) * projected[:, hidden_width:]).astype(
        jnp.bfloat16
    )
    return jnp.dot(hidden, weight_down, preferred_element_type=jnp.float32).astype(jnp.bfloat16)


def per_device(tokens, choices, gate_codes, hot_list, w_in, w_down):
    nexpert = lax.axis_size("expert")
    tok_rows, model_width = tokens.shape
    hot_rows = tok_rows // 8
    capacity = (2 * tok_rows - hot_rows + nexpert - 2) // (nexpert - 1)
    hot_id = hot_list[0]
    marked = choices == nexpert
    experts = jnp.where(marked, hot_id, choices)
    gate_vals = gate_codes.astype(jnp.float32) / 256.0
    own_in = w_in[0]
    own_down = w_down[0]
    slot_depth = max(capacity, hot_rows)
    routed = jnp.ones_like(marked)
    flat_exp = experts.reshape(-1)
    flat_use = routed.reshape(-1)
    lane_ids = jnp.arange(nexpert, dtype=jnp.int32)
    matches = flat_exp[:, None] == lane_ids[None, :]
    onehot = jnp.logical_and(matches, flat_use[:, None]).astype(jnp.int32)
    position = jnp.sum((jnp.cumsum(onehot, 0) - 1) * onehot, 1)
    slot_total = nexpert * slot_depth
    slot_ids = jnp.where(flat_use, flat_exp * slot_depth + position, slot_total)
    source_ids = jnp.arange(2 * tok_rows, dtype=jnp.int32) // 2
    buffer = jnp.zeros((slot_total, model_width), jnp.bfloat16)
    buffer = buffer.at[slot_ids].set(tokens[source_ids], mode="drop")
    outgoing = buffer.reshape(nexpert, slot_depth, model_width)
    arrived = lax.all_to_all(outgoing, "expert", split_axis=0, concat_axis=0, tiled=True)
    item_count = arrived.shape[1]
    finished = expert_rows(arrived.reshape(-1, model_width), own_in, own_down)
    finished = finished.reshape(nexpert, item_count, model_width)
    returned_rows = lax.all_to_all(finished, "expert", split_axis=0, concat_axis=0, tiled=True)
    results = returned_rows.reshape(slot_total, model_width)[jnp.minimum(slot_ids, slot_total - 1)]
    weights = jnp.where(flat_use, gate_vals.reshape(-1), 0.0)
    combined = (
        (weights[:, None] * results.astype(jnp.float32)).reshape(tok_rows, 2, model_width).sum(1)
    )
    mixed = combined.astype(jnp.bfloat16)
    local_counts = jnp.sum(matches.astype(jnp.float32), 0)
    totals = lax.psum(local_counts, ("dp", "expert"))
    mine = lax.dynamic_slice_in_dim(totals, lax.axis_index("expert"), 1)
    expert_load = mine / (2.0 * tok_rows * lax.axis_size("dp"))
    return (mixed, expert_load)


def solution(mesh):
    return jax.shard_map(
        per_device,
        mesh=mesh,
        in_specs=(
            P(("dp", "expert"), None),
            P(("dp", "expert"), None),
            P(("dp", "expert"), None),
            P("dp"),
            P("expert", None, None),
            P("expert", None, None),
        ),
        out_specs=(P(("dp", "expert"), None), P("expert")),
        check_vma=False,
    )
```

profile of v0, /device:TPU:0, one launch (start us, length us, event | category | flops | bytes accessed | tf_op | source)
XLA Modules:
  0.0 106.5 jit_solution(113277009087829135)
XLA Ops:
  0.6 0.0 copy-start
  1.4 0.7 broadcast_multiply_fusion
  2.1 0.1 copy.13
  2.2 0.1 eq.37
  2.4 0.1 eq.33
  2.5 1.2 %reduce-window.6 = s32[4,2,128]{2,1,0:T(2,128)S(1)} reduce-window(s32[4,2,128]{2,1,0:T(2,128)S(1)} %compare_convert_fusion, s32[]{:T(128)} %constant.44.clone.1), window={size=1x1x128 pad=0_0x0_0x127_0}, to_apply=%region_0.1 | reduce-window | flops 130048 | bytes 8196 | tf_op jit(solution)/shard_map/reduce-window
  3.8 0.1 slice.20
  3.9 0.1 copy.15
  4.0 0.1 copy.16
  4.1 0.1 add_bitcast_fusion
  4.2 0.1 copy.12
  4.3 0.1 mul.42
  4.5 5.9 %scatter_custom_fusion = bf16[320,2048]{1,0:T(8,128)(2,1)S(1)} fusion(s32[256]{0:T(256)S(1)} %bitcast.40, bf16[128,2048]{1,0:T(8,128)(2,1)} %param.6, s32[1024]{0:T(1024)S(1)} %pad_clamp_fusion.1, bf16[]{:T(256)} %constant.20.clone.1), kind=kCustom, calls=%fused_computation.8 | custom fusion | bytes 1311232 | tf_op jit(solution)/shard_map/scatter | solution.py:39
  10.4 21.3 %all_to_all.10 = bf16[4,80,2048]{2,1,0:T(8,128)(2,1)S(1)} all-to-all(bf16[4,80,2048]{2,1,0:T(8,128)(2,1)S(1)} %bitcast.33), channel_id=1, replica_groups=mesh['dp'=8,'expert'=4] {'expert'}, dimensions={0} | all-to-all | bytes 2621440 | tf_op jit(solution)/shard_map/all_to_all | solution.py:41
  31.7 3.7 %fusion = f32[320,1024]{1,0:T(8,128)S(1)} fusion(bf16[320,2048]{1,0:T(8,128)(2,1)S(1)} %bitcast.35, bf16[1,2048,1024]{2,1,0:T(8,128)(2,1)} %param.10), kind=kOutput, calls=%fused_computation.3 | convolution fusion | flops 1342177280 | bytes 6815744 | tf_op jit(solution)/shard_map/dot_general | solution.py:8
  35.4 2.0 %convolution_convert_fusion = bf16[320,2048]{1,0:T(8,128)(2,1)} fusion(bf16[1,512,2048]{2,1,0:T(8,128)(2,1)S(1)} %copy-done, f32[320,1024]{1,0:T(8,128)S(1)} %fusion), kind=kOutput, calls=%fused_computation.5 | convolution fusion | flops 672727040 | bytes 4718592 | tf_op jit(solution)/shard_map/dot_general | solution.py:13
  37.4 3.7 %all-to-all-start.1 = ((bf16[4,80,2048]{2,1,0:T(8,128)(2,1)}), bf16[4,80,2048]{2,1,0:T(8,128)(2,1)S(1)}, u32[]{:S(2)}, u32[]{:S(2)}) async-start(bf16[4,80,2048]{2,1,0:T(8,128)(2,1)} %bitcast.34), calls=%async_computation.1 | async-start | bytes 2621440 | tf_op jit(solution)/shard_map/all_to_all | solution.py:45
  41.0 0.1 convert_reduce_fusion
  41.2 51.5 %psum.7 = f32[4]{0:T(128)S(1)} all-reduce(f32[4]{0:T(128)S(1)} %convert_reduce_fusion), channel_id=1, replica_groups=mesh['dp'=8,'expert'=4] {'dp','expert'}, use_global_device_ids=true, to_apply=%region_6.7 | all-reduce | flops 4 | bytes 32 | tf_op jit(solution)/shard_map/psum | solution.py:53
  92.7 0.1 copy.11
  92.8 0.6 dynamic_slice.3
  94.0 2.3 %gather_fusion = bf16[256,2048]{1,0:T(8,128)(2,1)} fusion(bf16[320,2048]{1,0:T(8,128)(2,1)S(1)} %bitcast.32, s32[1024]{0:T(1024)S(1)} %pad_clamp_fusion), kind=kCustom, calls=%fused_computation.1 | custom fusion | bytes 2098176 | tf_op jit(solution)/shard_map/gather | solution.py:46
  96.4 3.4 %reshape.145 = f32[128,2,2048]{2,1,0:T(2,128)} reshape(bf16[256,2048]{1,0:T(8,128)(2,1)} %gather_fusion) | data formatting | bytes 3145728 | tf_op jit(solution)/shard_map/convert_element_type | solution.py:49
  99.8 5.6 %multiply_reduce_fusion = bf16[128,2048]{1,0:T(8,128)(2,1)} fusion(f32[128,2,2048]{2,1,0:T(2,128)} %reshape.145, f32[128,2]{1,0:T(8,128)S(1)} %copy.11), kind=kLoop, calls=%fused_computation.7 | loop fusion | flops 786432 | bytes 2622464 | tf_op jit(solution)/shard_map/reduce_sum | solution.py:49
  (13 shorter events, 0.1 us)
Async XLA Ops:
  0.6 34.8 %copy-start = (bf16[1,512,2048]{2,1,0:T(8,128)(2,1)S(1)}, bf16[1,512,2048]{2,1,0:T(8,128)(2,1)}, u32[]{:S(2)}) copy-start(bf16[1,512,2048]{2,1,0:T(8,128)(2,1)} %param.11) | copy-start | bytes 6291460
  37.4 55.3 %copy-start.1 = (s32[128,2]{0,1:T(2,128)S(1)}, s32[128,2]{0,1:T(2,128)}, u32[]{:S(2)}) copy-start(s32[128,2]{0,1:T(2,128)} %param.8) | copy-start | bytes 3076
  37.4 56.7 %all-to-all-start.1 = ((bf16[4,80,2048]{2,1,0:T(8,128)(2,1)}), bf16[4,80,2048]{2,1,0:T(8,128)(2,1)S(1)}, u32[]{:S(2)}, u32[]{:S(2)}) async-start(bf16[4,80,2048]{2,1,0:T(8,128)(2,1)} %bitcast.34), calls=%async_computation.1 | async-start | bytes 2621440 | tf_op jit(solution)/shard_map/all_to_all | solution.py:45
where the time goes:
time: 107 us
  blocking collectives  72.8 us (68%)
  local copies, waits for them, and re-layouts  13.3 us (12%)
  other arithmetic  7.79 us (7%)
  matrix products  5.69 us (5%)
  starting transfers between devices  3.67 us (3%)
  between operations  3.31 us (3%)
    psum x1, blocking collectives, per_device(): totals = lax.psum(local_counts, ('dp', 'expert'))  51.5 us
    all_to_all x1, blocking collectives, per_device(): lax.all_to_all(outgoing, 'expert', split_axis=0, concat_axis=0, tiled=True)  21.3 us
    scatter x1, local copies, waits for them, and re-layouts, per_device(): buffer = buffer.at[slot_ids].set(tokens[source_ids], mode='drop')  5.9 us
    reduce_sum x1, other arithmetic, per_device(): (weights[:, None] * results.astype(jnp.float32)).reshape(tok_rows, 2, mod...  5.59 us
    dot_general x1, matrix products, expert_rows(): jnp.dot(row_block, weight_in, preferred_element_type=jnp.float32)  3.73 us
    all_to_all x1, starting transfers between devices, per_device(): lax.all_to_all(finished, 'expert', split_axis=0, concat_axis=0, tiled=True)  3.67 us
    convert_element_type x1, local copies, waits for them, and re-layouts, per_device(): results.astype(jnp.float32)  3.39 us
    gather x1, local copies, waits for them, and re-layouts, per_device(): returned_rows.reshape(slot_total, model_width)  2.34 us
  transfers between devices with their start and end apart: 1, of which 0 were waited for; matrix products, arithmetic and copies ran while one was open for 1% of the time, Pallas kernels for 0%

commit v1 on v0

v1 whole, which is shorter than its diff:
```python
import functools

import jax
import jax.numpy as jnp
from jax import lax
from jax.experimental import pallas as pl
from jax.experimental.pallas import tpu as pltpu
from jax.sharding import PartitionSpec as P

MESH = pl.DeviceIdType.MESH
CHUNKS = 4


def moe_kernel(
    n, ndp, hot_ref, choices_ref, codes_ref, tokens_ref, w_in_ref, w_down_ref,
    out_ref, load_ref,
    xbuf, pbuf, rbuf, wbuf, wcol, hid, yown, acc, win, wdown, csend, crecv,
    load_sem, x_sem, xs_send, xs_recv, xf_send, xf_recv, ws_send, ws_recv,
    wf_send, wf_recv, p_send, p_recv, r_send, r_recv, c_send, c_recv,
):
    chips = n // 2
    rows, width = tokens_ref.shape
    part = rows // CHUNKS
    hidden_width = wdown.shape[0]
    dp, me = lax.axis_index("dp"), lax.axis_index("expert")
    chip, core = me // 2, me % 2
    sibling = (dp, chip * 2 + 1 - core)

    def away(d):
        return (dp, ((chip + d) % chips) * 2 + core)

    def back(d):
        return (dp, ((chip + chips - d) % chips) * 2 + core)

    dp_steps = []
    bit = 1
    while bit < ndp:
        dp_steps.append((dp + bit - 2 * bit * ((dp // bit) % 2), me))
        bit *= 2

    barrier = pltpu.get_barrier_semaphore()
    peers = [sibling] + [away(d) for d in range(1, chips)] + dp_steps
    for peer in peers:
        pl.semaphore_signal(barrier, inc=1, device_id=peer, device_id_type=MESH)

    fetch_in = pltpu.make_async_copy(w_in_ref.at[0], win, load_sem.at[0])
    fetch_down = pltpu.make_async_copy(w_down_ref.at[0], wdown, load_sem.at[1])

    def own_rows(c):
        return pltpu.make_async_copy(
            tokens_ref.at[pl.ds(c * part, part)], xbuf.at[0, c, 0], x_sem.at[c]
        )

    for c in range(CHUNKS):
        own_rows(c).start()
    fetch_in.start()
    fetch_down.start()

    choices = choices_ref[...]
    experts = jnp.where(choices == n, hot_ref[0], choices)
    gates = codes_ref[...].astype(jnp.float32) / 256.0
    padded = wbuf.shape[2]
    ids = lax.broadcasted_iota(jnp.int32, (padded, rows), 0)
    first, second = ids == experts[0:1], ids == experts[1:2]
    wbuf[0, 0] = jnp.where(first, gates[0:1], 0.0) + jnp.where(second, gates[1:2], 0.0)
    counts = jnp.sum(first.astype(jnp.float32) + second.astype(jnp.float32), 1, keepdims=True)
    csend[0] = jnp.broadcast_to(counts, csend.shape[1:])

    pl.semaphore_wait(barrier, len(peers))

    def remote(src, dst, send, recv, device):
        return pltpu.make_async_remote_copy(
            src_ref=src, dst_ref=dst, send_sem=send, recv_sem=recv,
            device_id=device, device_id_type=MESH,
        )

    def send_weights(d):
        return remote(wbuf.at[0, 0], wbuf.at[d, 0], ws_send.at[d], ws_recv.at[d], away(d))

    def pass_weights(d):
        return remote(wbuf.at[d, 0], wbuf.at[d, 1], wf_send.at[d], wf_recv.at[d], sibling)

    def send_rows(d, c):
        return remote(
            tokens_ref.at[pl.ds(c * part, part)], xbuf.at[d, c, 0],
            xs_send.at[d, c], xs_recv.at[d, c], away(d),
        )

    def pass_rows(d, c):
        return remote(
            xbuf.at[d, c, 0], xbuf.at[d, c, 1], xf_send.at[d, c], xf_recv.at[d, c], sibling
        )

    def own_pass(c):
        return remote(
            tokens_ref.at[pl.ds(c * part, part)], xbuf.at[0, c, 1],
            xf_send.at[0, c], xf_recv.at[0, c], sibling,
        )

    def send_partial(d, c):
        return remote(
            xbuf.at[d, c, 1], pbuf.at[d, c], p_send.at[d, c], p_recv.at[d, c], sibling
        )

    def send_result(d, c):
        return remote(
            xbuf.at[d, c, 0], rbuf.at[d, c], r_send.at[d, c], r_recv.at[d, c], back(d)
        )

    def send_counts(step, device):
        src = min(step, len(dp_steps) + 1)
        return remote(
            csend.at[src], crecv.at[step], c_send.at[step], c_recv.at[step], device
        )

    for d in range(1, chips):
        send_weights(d).start()
    pass_weights(0).start()
    for c in range(CHUNKS):
        for d in range(1, chips):
            send_rows(d, c).start()
    for c in range(CHUNKS):
        own_pass(c).start()

    count_steps = dp_steps + [sibling]
    send_counts(0, count_steps[0]).start()

    def column(d, j):
        row = wbuf[d, j, pl.ds(me, 1), :]
        wide = jnp.transpose(jnp.broadcast_to(row, (rows, rows)))
        for c in range(CHUNKS):
            wcol[d, c, j] = wide[c * part : (c + 1) * part]

    def hidden_of(block, total):
        step = min(256, hidden_width)

        @pl.loop(0, hidden_width // step)
        def _(t):
            at = pl.ds(pl.multiple_of(t * step, step), step)
            at_up = pl.ds(pl.multiple_of(hidden_width + t * step, step), step)
            x = block()
            gate = jnp.dot(x, win[:, at], preferred_element_type=jnp.float32)
            up = jnp.dot(x, win[:, at_up], preferred_element_type=jnp.float32)
            hid[0:total, at] = (jax.nn.silu(gate) * up).astype(jnp.bfloat16)

    def down_of(total, weight, store):
        step = min(256, width)

        @pl.loop(0, width // step)
        def _(t):
            at = pl.ds(pl.multiple_of(t * step, step), step)
            done = jnp.dot(hid[0:total], wdown[:, at], preferred_element_type=jnp.float32)
            done = done.astype(jnp.bfloat16).astype(jnp.float32)
            store(at, done * weight()[:, 0:1])

    column(0, 0)
    pass_weights(0).wait_recv()
    column(0, 1)
    for c in range(CHUNKS):
        own_rows(c).wait()
        own_pass(c).wait_recv()
    fetch_in.wait()
    hidden_of(lambda: xbuf[0].reshape(2 * rows, width), 2 * rows)
    fetch_down.wait()

    def store_own(at, y):
        y = y.reshape(CHUNKS, 2, part, y.shape[1])
        acc[:, :, at] = y[:, 0]
        for c in range(CHUNKS):
            xbuf[0, c, 1, :, at] = y[c, 1].astype(jnp.bfloat16)

    down_of(2 * rows, lambda: wcol[0].reshape(2 * rows, rows), store_own)
    for c in range(CHUNKS):
        send_partial(0, c).start()

    def share_counts(step):
        copy = send_counts(step, count_steps[step])
        copy.wait()
        csend[step + 1] = csend[step] + crecv[step]

    for step in range(len(count_steps)):
        share_counts(step)
        if step + 1 < len(count_steps):
            send_counts(step + 1, count_steps[step + 1]).start()
    chip_steps = [(len(count_steps) + d - 1, away(d)) for d in range(1, chips)]
    for step, device in chip_steps:
        send_counts(step, device).start()

    @pl.loop(1, chips)
    def _(d):
        send_weights(d).wait_recv()
        pass_weights(d).start()
        column(d, 0)
        pass_weights(d).wait_recv()
        column(d, 1)

    @pl.loop(0, CHUNKS * (chips - 1))
    def _(item):
        c, d = item // (chips - 1), 1 + item % (chips - 1)
        send_rows(d, c).wait_recv()
        pass_rows(d, c).start()
        pass_rows(d, c).wait_recv()
        hidden_of(lambda: xbuf[d, c].reshape(2 * part, width), 2 * part)

        def store(at, y):
            yown[:, at] = y[0:part]
            xbuf[d, c, 1, :, at] = y[part:].astype(jnp.bfloat16)

        down_of(2 * part, lambda: wcol[d, c].reshape(2 * part, rows), store)
        send_partial(d, c).start()
        pass_rows(d, c).wait_send()
        send_partial(d, c).wait_recv()
        xbuf[d, c, 0] = (yown[...] + pbuf[d, c].astype(jnp.float32)).astype(jnp.bfloat16)
        send_result(d, c).start()

    total = csend[len(count_steps)]
    for step, device in chip_steps:
        send_counts(step, device).wait()
        total = total + crecv[step]
    csend[len(count_steps)] = total
    load_ref[...] = csend[len(count_steps), pl.ds(me, 1), 0:1] / (2.0 * rows * ndp)

    for c in range(CHUNKS):
        send_partial(0, c).wait_recv()
        acc[c] = acc[c] + pbuf[0, c].astype(jnp.float32)
    for c in range(CHUNKS):

        @pl.loop(1, chips)
        def _(d):
            send_result(d, c).wait_recv()
            acc[c] = acc[c] + rbuf[d, c].astype(jnp.float32)

        out_ref[c * part : (c + 1) * part, :] = acc[c].astype(jnp.bfloat16)

    pass_weights(0).wait_send()
    for c in range(CHUNKS):
        own_pass(c).wait_send()
        send_partial(0, c).wait_send()

    @pl.loop(1, chips)
    def _(d):
        send_weights(d).wait_send()
        pass_weights(d).wait_send()
        for c in range(CHUNKS):
            send_rows(d, c).wait_send()
            send_partial(d, c).wait_send()
            send_result(d, c).wait_send()


def per_device(tokens, choices, gate_codes, hot_list, w_in, w_down):
    n, ndp = lax.axis_size("expert"), lax.axis_size("dp")
    rows, width = tokens.shape
    hidden_width = w_down.shape[1]
    chips, part = n // 2, rows // CHUNKS
    padded = -(-n // 8) * 8
    steps = (ndp - 1).bit_length() + 1
    bf16, f32 = jnp.bfloat16, jnp.float32
    dma = pltpu.SemaphoreType.DMA
    vmem = pl.BlockSpec(memory_space=pltpu.VMEM)
    mixed, load = pl.pallas_call(
        functools.partial(moe_kernel, n, ndp),
        out_shape=(
            jax.ShapeDtypeStruct((rows, width), bf16),
            jax.ShapeDtypeStruct((1, 1), f32),
        ),
        in_specs=[pl.BlockSpec(memory_space=pltpu.SMEM), vmem, vmem]
        + [pl.BlockSpec(memory_space=pl.ANY)] * 3,
        out_specs=(vmem, vmem),
        scratch_shapes=[
            pltpu.VMEM((chips, CHUNKS, 2, part, width), bf16),
            pltpu.VMEM((chips, CHUNKS, part, width), bf16),
            pltpu.VMEM((chips, CHUNKS, part, width), bf16),
            pltpu.VMEM((chips, 2, padded, rows), f32),
            pltpu.VMEM((chips, CHUNKS, 2, part, rows), f32),
            pltpu.VMEM((2 * rows, hidden_width), bf16),
            pltpu.VMEM((part, width), f32),
            pltpu.VMEM((CHUNKS, part, width), f32),
            pltpu.VMEM(w_in.shape[1:], bf16),
            pltpu.VMEM(w_down.shape[1:], bf16),
            pltpu.VMEM((steps + 1, padded, 128), f32),
            pltpu.VMEM((steps + chips - 1, padded, 128), f32),
            dma((2,)), dma((CHUNKS,)),
            dma((chips, CHUNKS)), dma((chips, CHUNKS)),
            dma((chips, CHUNKS)), dma((chips, CHUNKS)),
            dma((chips,)), dma((chips,)),
            dma((chips,)), dma((chips,)),
            dma((chips, CHUNKS)), dma((chips, CHUNKS)),
            dma((chips, CHUNKS)), dma((chips, CHUNKS)),
            dma((steps + chips - 1,)), dma((steps + chips - 1,)),
        ],
        compiler_params=pltpu.CompilerParams(
            collective_id=0, has_side_effects=True, vmem_limit_bytes=58 * 2**20
        ),
    )(hot_list, choices.T, gate_codes.T, tokens, w_in, w_down)
    return mixed, load.reshape(1)


def solution(mesh):
    return jax.shard_map(
        per_device,
        mesh=mesh,
        in_specs=(
            P(("dp", "expert"), None),
            P(("dp", "expert"), None),
            P(("dp", "expert"), None),
            P("dp"),
            P("expert", None, None),
            P("expert", None, None),
        ),
        out_specs=(P(("dp", "expert"), None), P("expert")),
        check_vma=False,
    )
```

time: 107 us -> 48.4 us (0.45)
  blocking collectives: 72.8 us -> 0 us
  Pallas kernels: 0 us -> 43.4 us
  local copies, waits for them, and re-layouts: 13.3 us -> 1.88 us
  other arithmetic: 7.79 us -> 0 us
  matrix products: 5.69 us -> 0 us
  starting transfers between devices: 3.67 us -> 0 us
    psum x1 -> x0, blocking collectives: 51.5 us -> none  [per_device(): totals = lax.psum(local_counts, ('dp', 'expert'))]
    pallas_call x0 -> x1, Pallas kernels: none -> 43.4 us  [per_device(): pl.pallas_call(functools.partial(moe_kernel, n, ndp), out_shape=(jax.Shap...]
    all_to_all x1 -> x0, blocking collectives: 21.3 us -> none  [per_device(): lax.all_to_all(outgoing, 'expert', split_axis=0, concat_axis=0, tiled=True)]
    scatter x1 -> x0, local copies, waits for them, and re-layouts: 5.9 us -> none  [per_device(): buffer = buffer.at[slot_ids].set(tokens[source_ids], mode='drop')]
    reduce_sum x3 -> x0, other arithmetic: 5.72 us -> none  [the longest x1 5.59 us: per_device(): (weights[:, None] * results.astype(jnp.float32)).reshape(tok_rows, 2, mod...]
    dot_general x2 -> x0, matrix products: 5.69 us -> none  [the longest x1 3.73 us: expert_rows(): jnp.dot(row_block, weight_in, preferred_element_type=jnp.float32)]
    all_to_all x1 -> x0, starting transfers between devices: 3.67 us -> none  [per_device(): lax.all_to_all(finished, 'expert', split_axis=0, concat_axis=0, tiled=True)]
    convert_element_type x1 -> x0, local copies, waits for them, and re-layouts: 3.39 us -> none  [per_device(): results.astype(jnp.float32)]
  transfers between devices with their start and end apart: 1 -> 0, of which waited for: 0 -> 0; matrix products, arithmetic and copies ran while one was open for 1% -> 0% of each run, Pallas kernels for 0% -> 0%
where the time goes in v1:
time: 48.4 us; the launch traced here: 48.2 us
  Pallas kernels  43.4 us (90%)
  between operations  2.98 us (6%)
  local copies, waits for them, and re-layouts  1.88 us (4%)
    pallas_call x1, Pallas kernels, per_device(): pl.pallas_call(functools.partial(moe_kernel, n, ndp), out_shape=(jax.Shap...  43.4 us
    unnamed x1, local copies, waits for them, and re-layouts  1.88 us

profile of v1, /device:TPU:0, one launch (start us, length us, event | category | flops | bytes accessed | tf_op | source)
XLA Modules:
  0.0 48.2 jit_solution(13864536936098220814)
XLA Ops:
  1.3 43.4 %shard_map.77 = (bf16[128,2048]{1,0:T(8,128)(2,1)}, f32[1,1]{1,0:T(1,128)}) custom-call(s32[1]{0:T(128)S(6)} %copy.10.hot_ref, s32[2,128]{1,0:T(2,128)} %bitcast.3, s32[2,128]{1,0:T(2,128)} %bitcast.4, bf16[128,2048]{1,0:T(8,128)(2,1)} %tokens_ref.1, bf16[1,2048,1024]{2,1,0:T(8,128)(2,1)} %w_in_ref.1, bf16[1,512,2048]{2,1,0:T(8,128)(2,1)} %w_down_ref.1), custom_call_target="tpu_custom_call" | custom-call | tf_op jit(solution)/shard_map/pallas_call | solution.py:260
  44.7 1.9 %copy.11 = bf16[128,2048]{1,0:T(8,128)(2,1)} copy(bf16[128,2048]{1,0:T(8,128)(2,1)} %get-tuple-element.8) | data formatting | bytes 1048576

commit v2 on v1

--- a/solution.py
+++ b/solution.py
@@ -125,6 +125,17 @@
     count_steps = dp_steps + [sibling]
     send_counts(0, count_steps[0]).start()
 
+    chip_steps = [(len(count_steps) + d - 1, away(d)) for d in range(1, chips)]
+
+    def share_counts(step):
+        send_counts(step, count_steps[step]).wait()
+        csend[step + 1] = csend[step] + crecv[step]
+        if step + 1 < len(count_steps):
+            send_counts(step + 1, count_steps[step + 1]).start()
+        else:
+            for later, device in chip_steps:
+                send_counts(later, device).start()
+
     def column(d, j):
         row = wbuf[d, j, pl.ds(me, 1), :]
         wide = jnp.transpose(jnp.broadcast_to(row, (rows, rows)))
@@ -134,7 +145,7 @@
     def hidden_of(block, total):
         step = min(256, hidden_width)
 
-        @pl.loop(0, hidden_width // step)
+        @pl.loop(0, hidden_width // step, unroll=True)
         def _(t):
             at = pl.ds(pl.multiple_of(t * step, step), step)
             at_up = pl.ds(pl.multiple_of(hidden_width + t * step, step), step)
@@ -146,7 +157,7 @@
     def down_of(total, weight, store):
         step = min(256, width)
 
-        @pl.loop(0, width // step)
+        @pl.loop(0, width // step, unroll=True)
         def _(t):
             at = pl.ds(pl.multiple_of(t * step, step), step)
             done = jnp.dot(hid[0:total], wdown[:, at], preferred_element_type=jnp.float32)
@@ -161,6 +172,7 @@
         own_pass(c).wait_recv()
     fetch_in.wait()
     hidden_of(lambda: xbuf[0].reshape(2 * rows, width), 2 * rows)
+    share_counts(0)
     fetch_down.wait()
 
     def store_own(at, y):
@@ -172,19 +184,8 @@
     down_of(2 * rows, lambda: wcol[0].reshape(2 * rows, rows), store_own)
     for c in range(CHUNKS):
         send_partial(0, c).start()
-
-    def share_counts(step):
-        copy = send_counts(step, count_steps[step])
-        copy.wait()
-        csend[step + 1] = csend[step] + crecv[step]
-
-    for step in range(len(count_steps)):
+    for step in range(1, min(2, len(count_steps))):
         share_counts(step)
-        if step + 1 < len(count_steps):
-            send_counts(step + 1, count_steps[step + 1]).start()
-    chip_steps = [(len(count_steps) + d - 1, away(d)) for d in range(1, chips)]
-    for step, device in chip_steps:
-        send_counts(step, device).start()
 
     @pl.loop(1, chips)
     def _(d):
@@ -194,11 +195,21 @@
         pass_weights(d).wait_recv()
         column(d, 1)
 
-    @pl.loop(0, CHUNKS * (chips - 1))
-    def _(item):
-        c, d = item // (chips - 1), 1 + item % (chips - 1)
+    items = CHUNKS * (chips - 1)
+
+    def place(item):
+        return 1 + item % (chips - 1), item // (chips - 1)
+
+    def hand_over(item):
+        d, c = place(item)
         send_rows(d, c).wait_recv()
         pass_rows(d, c).start()
+
+    hand_over(0)
+
+    @pl.loop(0, items)
+    def _(item):
+        d, c = place(item)
         pass_rows(d, c).wait_recv()
         hidden_of(lambda: xbuf[d, c].reshape(2 * part, width), 2 * part)
 
@@ -208,11 +219,21 @@
 
         down_of(2 * part, lambda: wcol[d, c].reshape(2 * part, rows), store)
         send_partial(d, c).start()
+
+        @pl.when(item + 1 < items)
+        def _():
+            hand_over(item + 1)
+
         pass_rows(d, c).wait_send()
         send_partial(d, c).wait_recv()
         xbuf[d, c, 0] = (yown[...] + pbuf[d, c].astype(jnp.float32)).astype(jnp.bfloat16)
         send_result(d, c).start()
 
+    for c in range(CHUNKS):
+        send_partial(0, c).wait_recv()
+        acc[c] = acc[c] + pbuf[0, c].astype(jnp.float32)
+    for step in range(min(2, len(count_steps)), len(count_steps)):
+        share_counts(step)
     total = csend[len(count_steps)]
     for step, device in chip_steps:
         send_counts(step, device).wait()
@@ -220,9 +241,6 @@
     csend[len(count_steps)] = total
     load_ref[...] = csend[len(count_steps), pl.ds(me, 1), 0:1] / (2.0 * rows * ndp)
 
-    for c in range(CHUNKS):
-        send_partial(0, c).wait_recv()
-        acc[c] = acc[c] + pbuf[0, c].astype(jnp.float32)
     for c in range(CHUNKS):
 
         @pl.loop(1, chips)

time: 48.4 us -> 36.3 us (0.75)
  Pallas kernels: 43.4 us -> 31.2 us
    pallas_call x1, Pallas kernels: 43.4 us -> 31.2 us  [per_device(): pl.pallas_call(functools.partial(moe_kernel, n, ndp), out_shape=(jax.Shap...]
where the time goes in v2:
time: 36.3 us; the launch traced here: 36.1 us
  Pallas kernels  31.2 us (86%)
  between operations  2.98 us (8%)
  local copies, waits for them, and re-layouts  1.88 us (5%)
    pallas_call x1, Pallas kernels, per_device(): pl.pallas_call(functools.partial(moe_kernel, n, ndp), out_shape=(jax.Shap...  31.2 us
    unnamed x1, local copies, waits for them, and re-layouts  1.88 us

profile of v2, /device:TPU:0, one launch (start us, length us, event | category | flops | bytes accessed | tf_op | source)
XLA Modules:
  0.0 36.1 jit_solution(12471592680528785610)
XLA Ops:
  1.3 31.2 %shard_map.77 = (bf16[128,2048]{1,0:T(8,128)(2,1)}, f32[1,1]{1,0:T(1,128)}) custom-call(s32[1]{0:T(128)S(6)} %copy.10.hot_ref, s32[2,128]{1,0:T(2,128)} %bitcast.3, s32[2,128]{1,0:T(2,128)} %bitcast.4, bf16[128,2048]{1,0:T(8,128)(2,1)} %tokens_ref.1, bf16[1,2048,1024]{2,1,0:T(8,128)(2,1)} %w_in_ref.1, bf16[1,512,2048]{2,1,0:T(8,128)(2,1)} %w_down_ref.1), custom_call_target="tpu_custom_call" | custom-call | tf_op jit(solution)/shard_map/pallas_call | solution.py:278
  32.5 1.9 %copy.11 = bf16[128,2048]{1,0:T(8,128)(2,1)} copy(bf16[128,2048]{1,0:T(8,128)(2,1)} %get-tuple-element.8) | data formatting | bytes 1048576

commit v3 on v2

--- a/solution.py
+++ b/solution.py
@@ -66,6 +66,8 @@
     counts = jnp.sum(first.astype(jnp.float32) + second.astype(jnp.float32), 1, keepdims=True)
     csend[0] = jnp.broadcast_to(counts, csend.shape[1:])
 
+    for c in range(CHUNKS):
+        own_rows(c).wait()
     pl.semaphore_wait(barrier, len(peers))
 
     def remote(src, dst, send, recv, device):
@@ -82,7 +84,7 @@
 
     def send_rows(d, c):
         return remote(
-            tokens_ref.at[pl.ds(c * part, part)], xbuf.at[d, c, 0],
+            xbuf.at[0, c, 0], xbuf.at[d, c, 0],
             xs_send.at[d, c], xs_recv.at[d, c], away(d),
         )
 
@@ -93,7 +95,7 @@
 
     def own_pass(c):
         return remote(
-            tokens_ref.at[pl.ds(c * part, part)], xbuf.at[0, c, 1],
+            xbuf.at[0, c, 0], xbuf.at[0, c, 1],
             xf_send.at[0, c], xf_recv.at[0, c], sibling,
         )
 
@@ -113,6 +115,8 @@
             csend.at[src], crecv.at[step], c_send.at[step], c_recv.at[step], device
         )
 
+    count_steps = dp_steps + [sibling]
+    send_counts(0, count_steps[0]).start()
     for d in range(1, chips):
         send_weights(d).start()
     pass_weights(0).start()
@@ -121,9 +125,6 @@
             send_rows(d, c).start()
     for c in range(CHUNKS):
         own_pass(c).start()
-
-    count_steps = dp_steps + [sibling]
-    send_counts(0, count_steps[0]).start()
 
     chip_steps = [(len(count_steps) + d - 1, away(d)) for d in range(1, chips)]
 
@@ -168,7 +169,6 @@
     pass_weights(0).wait_recv()
     column(0, 1)
     for c in range(CHUNKS):
-        own_rows(c).wait()
         own_pass(c).wait_recv()
     fetch_in.wait()
     hidden_of(lambda: xbuf[0].reshape(2 * rows, width), 2 * rows)
@@ -220,6 +220,9 @@
         down_of(2 * part, lambda: wcol[d, c].reshape(2 * part, rows), store)
         send_partial(d, c).start()
 
+        for step in range(2, min(2 + items, len(count_steps))):
+            pl.when(item == step - 2)(functools.partial(share_counts, step))
+
         @pl.when(item + 1 < items)
         def _():
             hand_over(item + 1)
@@ -232,7 +235,7 @@
     for c in range(CHUNKS):
         send_partial(0, c).wait_recv()
         acc[c] = acc[c] + pbuf[0, c].astype(jnp.float32)
-    for step in range(min(2, len(count_steps)), len(count_steps)):
+    for step in range(2 + items, len(count_steps)):
         share_counts(step)
     total = csend[len(count_steps)]
     for step, device in chip_steps:

time: 36.3 us -> 36.1 us (level)
  no operation moved by 1% of the time
where the time goes in v3:
time: 36.1 us; the launch traced here: 35.8 us
  Pallas kernels  31 us (86%)
  between operations  2.98 us (8%)
  local copies, waits for them, and re-layouts  1.88 us (5%)
    pallas_call x1, Pallas kernels, per_device(): pl.pallas_call(functools.partial(moe_kernel, n, ndp), out_shape=(jax.Shap...  31 us
    unnamed x1, local copies, waits for them, and re-layouts  1.88 us

profile of v3, /device:TPU:0, one launch (start us, length us, event | category | flops | bytes accessed | tf_op | source)
XLA Modules:
  0.0 35.8 jit_solution(18432237918383731251)
XLA Ops:
  1.3 31.0 %shard_map.77 = (bf16[128,2048]{1,0:T(8,128)(2,1)}, f32[1,1]{1,0:T(1,128)}) custom-call(s32[1]{0:T(128)S(6)} %copy.10.hot_ref, s32[2,128]{1,0:T(2,128)} %bitcast.3, s32[2,128]{1,0:T(2,128)} %bitcast.4, bf16[128,2048]{1,0:T(8,128)(2,1)} %tokens_ref.1, bf16[1,2048,1024]{2,1,0:T(8,128)(2,1)} %w_in_ref.1, bf16[1,512,2048]{2,1,0:T(8,128)(2,1)} %w_down_ref.1), custom_call_target="tpu_custom_call" | custom-call | tf_op jit(solution)/shard_map/pallas_call | solution.py:281
  32.3 1.9 %copy.11 = bf16[128,2048]{1,0:T(8,128)(2,1)} copy(bf16[128,2048]{1,0:T(8,128)(2,1)} %get-tuple-element.8) | data formatting | bytes 1048576
